TPU v7x, 32 devices: a whole 2x2x4 slice. The times are simulated.
32 devices in a mesh: groups: 2 (over y), tile: 4 (over x, core), cuts: 4 (over z).
Axes of the slice: x: 2, y: 2, z: 4, core: 2. Of those that a mesh axis runs over, the one named last changes fastest.
Arguments:
- trade: bfloat16 [16, 4, 256, 8192], P(('groups', 'cuts'), 'tile'), parts along dimension 0, may hold values from -6 to 6
- factor: bfloat16 [32768, 256], P(('groups', 'tile', 'cuts')), parts along dimension 0, may hold values from -0.375 to 0.375
- scales: float32 [16, 256], P(('groups', 'cuts')), parts along dimension 0, may hold values from 0.1 to 1.9
- core: float32 [512, 256], P('groups'), parts along dimension 0, may hold values from -4 to 4
Outputs:
- grad_factor: float32 [32768, 256], P(('groups', 'tile', 'cuts')), parts along dimension 0
- grad_window: float32 [1024, 256], P(('groups', 'cuts')), parts along dimension 0
- grad_core: float32 [512, 256], P('groups'), parts along dimension 0
- grad_scales: float32 [16, 256], P(('groups', 'cuts')), parts along dimension 0
There are 2 independent parts, one for each index of `groups`. A program takes and returns all parts, laid end to end along the dimension named above; each array names one. Nothing has to cross between parts.
All inputs are finite; a program needn't handle non-finite values.
Results may differ from a plain program's by a relative error of at most 0.00055.
Values may be sent and summed in bfloat16 or wider, within the bound.
A program may use at most 128 MiB of HBM per device.

v0:
```python
import math
import jax
import jax.numpy as jnp
from jax import lax
from jax.sharding import PartitionSpec as P

P_SIZE = 256


def swapped(value, axis, distance):
    mask = 2**distance
    pairs = [(source, source ^ mask) for source in range(lax.axis_size(axis))]
    return lax.ppermute(value, axis, pairs)


def from_root(block, axis, source):
    block = jnp.where(lax.axis_index(axis) == source, block, jnp.zeros_like(block))
    return lax.psum(block, axis)


def body(trade, factor, scales, core):
    n_cuts = lax.axis_size("cuts")
    band_index = lax.axis_index("tile") % 2
    months = trade.shape[0]
    rows_band = trade.shape[2]
    window_size = 2 * rows_band
    highest = lax.Precision.HIGHEST
    own_block = lax.all_gather(factor, "cuts", axis=0, tiled=True)
    block = own_block.shape[0]
    partner_block = swapped(own_block, "tile", 0)
    first_block = jnp.where(band_index == 0, own_block, partner_block)
    second_block = jnp.where(band_index == 0, partner_block, own_block)
    column_factor = jnp.concatenate([first_block, second_block], 0)
    window_block = from_root(own_block, "tile", 0)
    window_rows = lax.dynamic_slice_in_dim(window_block, band_index * rows_band, rows_band, 0)
    window32 = window_rows.astype(jnp.float32)
    coef = 1.0 / math.sqrt(months * n_cuts * window_size)
    acc_columns = jnp.zeros((2 * block, P_SIZE), jnp.float32)
    acc_window = jnp.zeros((rows_band, P_SIZE), jnp.float32)
    acc_core = jnp.zeros((P_SIZE, P_SIZE), jnp.float32)
    diag_terms = []
    for month in range(months):
        diag_k = scales[month]
        inner = diag_k[:, None] * core * diag_k[None, :]
        mapped = jnp.dot(window32, inner, precision=highest).astype(jnp.bfloat16)
        model = lax.dot_general(
            mapped, column_factor, (((1,), (1,)), ((), ())), preferred_element_type=jnp.float32
        )
        residual = (trade[month, 0].astype(jnp.float32) - model).astype(jnp.bfloat16)
        acc_columns = acc_columns + lax.dot_general(
            residual, mapped, (((0,), (0,)), ((), ())), preferred_element_type=jnp.float32
        )
        projected = jnp.dot(residual, column_factor, preferred_element_type=jnp.float32)
        acc_window = acc_window + jnp.dot(projected, inner.T, precision=highest)
        gram = jnp.dot(window32.T, projected, precision=highest)
        acc_core = acc_core + diag_k[:, None] * gram * diag_k[None, :]
        weighted = gram * core
        diag_terms.append(
            jnp.dot(weighted, diag_k, precision=highest)
            + jnp.dot(weighted.T, diag_k, precision=highest)
        )
    diag_stack = jnp.stack(diag_terms, 0)
    halves = acc_columns.reshape(2, block, P_SIZE)
    mine = jnp.where(band_index == 0, halves[0], halves[1])
    other = jnp.where(band_index == 0, halves[1], halves[0])
    received = swapped(other, "tile", 0)
    grad_factor = lax.psum_scatter(mine + received, "cuts", scatter_dimension=0, tiled=True)
    padded = lax.dynamic_update_slice_in_dim(
        jnp.zeros((window_size, P_SIZE), jnp.float32), acc_window, band_index * rows_band, 0
    )
    window_part = lax.psum_scatter(padded, "cuts", scatter_dimension=0, tiled=True)
    window_total = lax.psum(window_part, "tile")
    core_total = lax.psum(acc_core, ("tile", "cuts"))
    diag_total = lax.psum(diag_stack, "tile")
    return (-coef * grad_factor, -coef * window_total, -coef * core_total, -coef * diag_total)


def solution(mesh):
    return jax.shard_map(
        body,
        mesh=mesh,
        in_specs=(
            P(("groups", "cuts"), "tile", None, None),
            P(("groups", "tile", "cuts"), None),
            P(("groups", "cuts"), None),
            P("groups", None),
        ),
        out_specs=(
            P(("groups", "tile", "cuts"), None),
            P(("groups", "cuts"), None),
            P("groups", None),
            P(("groups", "cuts"), None),
        ),
        check_vma=False,
    )
```

profile of v0, /device:TPU:0, one launch (start us, length us, event | category | flops | bytes accessed | tf_op | source)
XLA Modules:
  0.0 385.2 jit_solution(4281532647967686441)
XLA Ops:
  7.2 0.7 all-gather.2.cloned.1.call-update
  7.9 50.3 %all-gather.2.cloned.1.call-done = bf16[4096,256]{1,0:T(8,128)(2,1)} async-done(((bf16[1024,256]{1,0:T(8,128)(2,1)}), bf16[4096,256]{1,0:T(8,128)(2,1)}) %all-gather.2.cloned.1.call-update) | async-done | bytes 2097168 | tf_op jit(solution)/shard_map/all_gather | solution.py:28
  58.2 4.5 %collective-permute-done = bf16[4096,256]{1,0:T(8,128)(2,1)} collective-permute-done((bf16[4096,256]{1,0:T(8,128)(2,1)}, bf16[4096,256]{1,0:T(8,128)(2,1)}, u32[]{:S(2)}, u32[]{:S(2)}) %collective-permute-start) | collective-permute-done | bytes 2097184 | tf_op jit(solution)/shard_map/ppermute | solution.py:13
  62.7 4.6 %broadcast_select_fusion.2 = (bf16[4096,256]{1,0:T(8,128)(2,1)S(1)}, bf16[4096,256]{1,0:T(8,128)(2,1)}, bf16[4096,256]{1,0:T(8,128)(2,1)}) fusion(bf16[4096,256]{1,0:T(8,128)(2,1)} %all-gather.2.cloned.1.call-done, bf16[4096,256]{1,0:T(8,128)(2,1)} %collective-permute-done, pred[]{:T(512)S(6)} %eq.6, pred[]{:T(512)S(6)} %eq.12), kind=kLoop, calls=%fused_computation.10 | loop fusion | flops 3145728 | bytes 10485762 | tf_op jit(solution)/shard_map/jit(_where)/select_n | solution.py:31
  67.5 50.2 %all-reduce.4.cloned.1.call-done = bf16[4096,256]{1,0:T(8,128)(2,1)} async-done(((bf16[4096,256]{1,0:T(8,128)(2,1)}), bf16[4096,256]{1,0:T(8,128)(2,1)}) %all-reduce.4.cloned.1.call-update) | async-done | bytes 2097168 | tf_op jit(solution)/shard_map/psum | solution.py:18
  117.6 1.3 convolution_convert_fusion.1
  119.0 4.3 %fusion = bf16[256,8192]{1,0:T(8,128)(2,1)S(1)} fusion(bf16[256,256]{1,0:T(8,128)(2,1)S(1)} %convolution_convert_fusion.1, bf16[2,1,256,8192]{3,2,1,0:T(8,128)(2,1)} %param.4, bf16[4096,256]{1,0:T(8,128)(2,1)} %get-tuple-element.5, bf16[4096,256]{1,0:T(8,128)(2,1)S(1)} %get-tuple-element.4), kind=kOutput, calls=%fused_computation.3 | convolution fusion | flops 1088421888 | bytes 12713984 | tf_op jit(solution)/shard_map/dot_general | solution.py:46
  123.2 1.5 convolution_convert_fusion
  124.7 9.6 %fusion.1 = bf16[256,8192]{1,0:T(8,128)(2,1)S(1)} fusion(bf16[256,256]{1,0:T(8,128)(2,1)S(1)} %convolution_convert_fusion, bf16[2,1,256,8192]{3,2,1,0:T(8,128)(2,1)} %param.4, bf16[4096,256]{1,0:T(8,128)(2,1)S(1)} %copy-done.6, bf16[4096,256]{1,0:T(8,128)(2,1)S(1)} %get-tuple-element.4), kind=kOutput, calls=%fused_computation.4 | convolution fusion | flops 1088421888 | bytes 12713984 | tf_op jit(solution)/shard_map/dot_general | solution.py:46
  134.4 1.3 fusion.43
  135.7 0.6 copy-done.2
  136.3 1.3 convolution_add_fusion
  137.7 2.8 slice_select_fusion
  140.5 1.6 copy-done
  142.2 4.2 %fusion.41 = f32[256,256]{1,0:T(8,128)S(1)} fusion(bf16[256,8192]{1,0:T(8,128)(2,1)} %copy-done.4, bf16[4096,256]{1,0:T(8,128)(2,1)} %get-tuple-element.5, bf16[4096,256]{1,0:T(8,128)(2,1)S(1)} %get-tuple-element.4), kind=kOutput, calls=%fused_computation.61 | convolution fusion | flops 1082130432 | bytes 8650752 | tf_op jit(solution)/shard_map/dot_general | solution.py:53
  146.4 0.5 fusion.7
  146.9 1.2 fusion.40
  148.2 0.5 fusion.2
  148.7 0.8 copy-done.5
  149.6 1.2 fusion.24
  150.8 1.9 multiply_add_fusion
  152.8 18.8 %reduce-scatter.5.cloned.1.call-done = f32[128,256]{1,0:T(8,128)} async-done(((f32[512,256]{1,0:T(8,128)}), f32[128,256]{1,0:T(8,128)}) %reduce-scatter.5.cloned.1.call-update) | async-done | bytes 131088 | tf_op jit(solution)/shard_map/reduce_scatter | solution.py:71
  171.7 7.4 %select_add_fusion = f32[4096,256]{1,0:T(8,128)} fusion(f32[4096,256]{1,0:T(8,128)} %collective-permute-done.1, f32[8192,256]{1,0:T(8,128)} %copy-done, pred[]{:T(512)S(6)} %eq.6), kind=kLoop, calls=%fused_computation.6 | loop fusion | flops 2097152 | bytes 16777216 | tf_op jit(solution)/shard_map/add | solution.py:67
  179.6 0.3 fusion.17
  180.3 5.7 %psum.31 = f32[2,256]{1,0:T(2,128)S(1)} all-reduce(f32[2,256]{1,0:T(2,128)S(1)} %pad_maximum_fusion.1), channel_id=1, replica_groups=mesh['groups'=2,'tile'=4,'cuts'=4] {'tile'}, use_global_device_ids=true, to_apply=%region_5.6 | all-reduce | flops 512 | bytes 4096 | tf_op jit(solution)/shard_map/psum | solution.py:74
  185.9 0.6 broadcast_multiply_fusion.3
  186.5 76.4 %all-reduce.8.cloned.1.call-done = f32[256,256]{1,0:T(8,128)} async-done(((f32[256,256]{1,0:T(8,128)}), f32[256,256]{1,0:T(8,128)}) %all-reduce.8.cloned.1.call-update) | async-done | bytes 262160 | tf_op jit(solution)/shard_map/psum | solution.py:73
  262.9 1.7 broadcast_multiply_fusion.1
  264.6 32.5 %all-reduce.6.cloned.1.call-done = f32[128,256]{1,0:T(8,128)} async-done(((f32[128,256]{1,0:T(8,128)}), f32[128,256]{1,0:T(8,128)}) %all-reduce.6.cloned.1.call-update) | async-done | bytes 131088 | tf_op jit(solution)/shard_map/psum | solution.py:72
  297.1 1.6 broadcast_multiply_fusion.2
  298.7 77.4 %reduce-scatter.3.cloned.1.call-done = f32[1024,256]{1,0:T(8,128)} async-done(((f32[4096,256]{1,0:T(8,128)}), f32[1024,256]{1,0:T(8,128)}) %reduce-scatter.3.cloned.1.call-update) | async-done | bytes 1048592 | tf_op jit(solution)/shard_map/reduce_scatter | solution.py:67
  376.1 2.3 broadcast_multiply_fusion
  (37 shorter events, 1.3 us)
Async XLA Ops:
  7.2 51.1 %all-gather.2.cloned.1.call-start = ((), (), s32[]{:S(2)}) async-start(), calls=%async_computation.2 | async-start | bytes 2621440 | tf_op jit(solution)/shard_map/all_gather | solution.py:28
  7.9 109.7 %all-reduce.4.cloned.1.call-start = ((), (), s32[]{:S(2)}) async-start(), calls=%async_computation.3 | async-start | bytes 4194304 | tf_op jit(solution)/shard_map/psum | solution.py:18
  58.2 4.5 %collective-permute-start = (bf16[4096,256]{1,0:T(8,128)(2,1)}, bf16[4096,256]{1,0:T(8,128)(2,1)}, u32[]{:S(2)}, u32[]{:S(2)}) collective-permute-start(bf16[4096,256]{1,0:T(8,128)(2,1)} %all-gather.2.cloned.1.call-done), channel_id=1, source_target_pairs={{0,4},{4,0},{8,12},{12,8},{1,5},{5,1},{9,13},{13,9},{2,6},{6,2},{1... | collective-permute-start | bytes 6291464 | tf_op jit(solution)/shard_map/ppermute | solution.py:13
  58.2 9.2 %copy-start.8 = (f32[2,256]{1,0:T(2,128)S(1)}, f32[2,256]{1,0:T(2,128)}, u32[]{:S(2)}) copy-start(f32[2,256]{1,0:T(2,128)} %param.6) | copy-start | bytes 6148
  58.2 59.4 %copy-start.1 = (f32[256,256]{1,0:T(8,128)S(1)}, f32[256,256]{1,0:T(8,128)}, u32[]{:S(2)}) copy-start(f32[256,256]{1,0:T(8,128)} %param.7) | copy-start | bytes 786436
  67.4 104.2 %reduce-scatter.5.cloned.1.call-start = ((), (), s32[]{:S(2)}) async-start(), calls=%async_computation.5 | async-start | bytes 655360 | tf_op jit(solution)/shard_map/reduce_scatter | solution.py:71
  118.9 5.8 %copy-start.6 = (bf16[4096,256]{1,0:T(8,128)(2,1)S(1)}, bf16[4096,256]{1,0:T(8,128)(2,1)}, u32[]{:S(2)}) copy-start(bf16[4096,256]{1,0:T(8,128)(2,1)} %get-tuple-element.5) | copy-start | bytes 6291460
  123.2 11.1 %copy-start.4 = (bf16[256,8192]{1,0:T(8,128)(2,1)}, bf16[256,8192]{1,0:T(8,128)(2,1)S(1)}, u32[]{:S(2)}) copy-start(bf16[256,8192]{1,0:T(8,128)(2,1)S(1)} %fusion) | copy-start | bytes 12582916
  134.4 2.0 copy-start.2
  137.7 4.5 %copy-start = (f32[8192,256]{1,0:T(8,128)}, f32[8192,256]{1,0:T(8,128)S(1)}, u32[]{:S(2)}) copy-start(f32[8192,256]{1,0:T(8,128)S(1)} %convolution_add_fusion) | copy-start | bytes 25165828
  142.2 29.5 %collective-permute-start.1 = (f32[4096,256]{1,0:T(8,128)}, f32[4096,256]{1,0:T(8,128)}, u32[]{:S(2)}, u32[]{:S(2)}) collective-permute-start(f32[4096,256]{1,0:T(8,128)} %slice_select_fusion), channel_id=1, source_target_pairs={{0,4},{4,0},{8,12},{12,8},{1,5},{5,1},{9,13},{13,9},{2,6},{6,2},{1... | collective-permute-start | bytes 12582920 | tf_op jit(solution)/shard_map/ppermute | solution.py:13
  142.2 4.7 %copy-start.3 = (bf16[256,8192]{1,0:T(8,128)(2,1)S(1)}, bf16[256,8192]{1,0:T(8,128)(2,1)}, u32[]{:S(2)}) copy-start(bf16[256,8192]{1,0:T(8,128)(2,1)} %copy-done.2) | copy-start | bytes 12582916
  142.2 4.8 %copy-start.7 = (bf16[4096,256]{1,0:T(8,128)(2,1)S(1)}, bf16[4096,256]{1,0:T(8,128)(2,1)}, u32[]{:S(2)}) copy-start(bf16[4096,256]{1,0:T(8,128)(2,1)} %get-tuple-element.5) | copy-start | bytes 6291460
  148.7 0.8 copy-start.5
  149.5 113.4 %all-reduce.8.cloned.1.call-start = ((), (), s32[]{:S(2)}) async-start(), calls=%async_computation.7 | async-start | bytes 524288 | tf_op jit(solution)/shard_map/psum | solution.py:73
  152.8 144.3 %all-reduce.6.cloned.1.call-start = ((), (), s32[]{:S(2)}) async-start(), calls=%async_computation.6 | async-start | bytes 262144 | tf_op jit(solution)/shard_map/psum | solution.py:72
  171.6 204.5 %reduce-scatter.3.cloned.1.call-start = ((), (), s32[]{:S(2)}) async-start(), calls=%async_computation.4 | async-start | bytes 5242880 | tf_op jit(solution)/shard_map/reduce_scatter | solution.py:67
Sparse Core Ops, SparseCore 0:
  9.6 48.6 all-gather.1
  67.5 50.0 all-reduce.3
  149.7 21.8 reduce-scatter.4
  175.8 87.1 all-reduce.7
  265.2 31.8 all-reduce.5
  299.3 76.7 reduce-scatter.2
where the time goes:
time: 385 us
  waiting for transfers between devices  311 us (81%)
  matrix products  30 us (8%)
  other arithmetic  21 us (5%)
  between operations  14.3 us (4%)
  blocking collectives  5.67 us (1%)
    reduce_scatter x1, waiting for transfers between devices, body(): lax.psum_scatter(mine + received, 'cuts', scatter_dimension=0, tiled=True)  77.4 us
    psum x1, waiting for transfers between devices, body(): core_total = lax.psum(acc_core, ('tile', 'cuts'))  76.4 us
    all_gather x1, waiting for transfers between devices, body(): own_block = lax.all_gather(factor, 'cuts', axis=0, tiled=True)  50.3 us
    psum x1, waiting for transfers between devices, from_root(): return lax.psum(block, axis)  50.2 us
    psum x1, waiting for transfers between devices, body(): window_total = lax.psum(window_part, 'tile')  32.5 us
    reduce_scatter x1, waiting for transfers between devices, body(): lax.psum_scatter(padded, 'cuts', scatter_dimension=0, tiled=True)  18.8 us
    dot_general x2, matrix products, body(): lax.dot_general(mapped, column_factor, (((1,), (1,)), ((), ())), preferre...  13.9 us
  transfers between devices with their start and end apart: 8, of which 7 were waited for; matrix products, arithmetic and copies ran while one was open for 6% of the time, Pallas kernels for 0%

commit v1 on v0

--- a/solution.py
+++ b/solution.py
@@ -70,7 +70,7 @@
     )
     window_part = lax.psum_scatter(padded, "cuts", scatter_dimension=0, tiled=True)
     window_total = lax.psum(window_part, "tile")
-    core_total = lax.psum(acc_core, ("tile", "cuts"))
+    core_total = lax.psum(lax.psum(acc_core, "cuts"), "tile")
     diag_total = lax.psum(diag_stack, "tile")
     return (-coef * grad_factor, -coef * window_total, -coef * core_total, -coef * diag_total)
 

time: 385 us -> 332 us (0.86)
  waiting for transfers between devices: 311 us -> 258 us
    psum x1, waiting for transfers between devices: 76.4 us -> 33.6 us  [body(): core_total = lax.psum(lax.psum(acc_core, 'cuts'), 'tile')]
    psum x1, waiting for transfers between devices: 32.5 us -> 18.3 us  [body(): window_total = lax.psum(window_part, 'tile')]
    reduce_scatter x1, waiting for transfers between devices: 18.8 us -> 24.1 us  [body(): lax.psum_scatter(padded, 'cuts', scatter_dimension=0, tiled=True)]
  transfers between devices with their start and end apart: 8 -> 8, of which waited for: 7 -> 7; matrix products, arithmetic and copies ran while one was open for 6% -> 7% of each run, Pallas kernels for 0% -> 0%
where the time goes in v1:
time: 332 us
  waiting for transfers between devices  258 us (78%)
  matrix products  29.8 us (9%)
  other arithmetic  21 us (6%)
  between operations  14.3 us (4%)
  blocking collectives  5.68 us (2%)
    reduce_scatter x1, waiting for transfers between devices, body(): lax.psum_scatter(mine + received, 'cuts', scatter_dimension=0, tiled=True)  75.8 us
    all_gather x1, waiting for transfers between devices, body(): own_block = lax.all_gather(factor, 'cuts', axis=0, tiled=True)  50.3 us
    psum x1, waiting for transfers between devices, from_root(): return lax.psum(block, axis)  50.2 us
    psum x1, waiting for transfers between devices, body(): core_total = lax.psum(lax.psum(acc_core, 'cuts'), 'tile')  33.6 us
    reduce_scatter x1, waiting for transfers between devices, body(): lax.psum_scatter(padded, 'cuts', scatter_dimension=0, tiled=True)  24.1 us
    psum x1, waiting for transfers between devices, body(): window_total = lax.psum(window_part, 'tile')  18.3 us
    dot_general x2, matrix products, body(): lax.dot_general(mapped, column_factor, (((1,), (1,)), ((), ())), preferre...  13.7 us
    add x1, other arithmetic, body(): mine + received  7.4 us
  transfers between devices with their start and end apart: 8, of which 7 were waited for; matrix products, arithmetic and copies ran while one was open for 7% of the time, Pallas kernels for 0%

profile of v1, /device:TPU:0, one launch (start us, length us, event | category | flops | bytes accessed | tf_op | source)
XLA Modules:
  0.0 332.0 jit_solution(6907211747240615153)
XLA Ops:
  7.2 0.7 all-gather.2.cloned.1.call-update
  7.9 50.3 %all-gather.2.cloned.1.call-done = bf16[4096,256]{1,0:T(8,128)(2,1)} async-done(((bf16[1024,256]{1,0:T(8,128)(2,1)}), bf16[4096,256]{1,0:T(8,128)(2,1)}) %all-gather.2.cloned.1.call-update) | async-done | bytes 2097168 | tf_op jit(solution)/shard_map/all_gather | solution.py:28
  58.2 4.5 %collective-permute-done = bf16[4096,256]{1,0:T(8,128)(2,1)} collective-permute-done((bf16[4096,256]{1,0:T(8,128)(2,1)}, bf16[4096,256]{1,0:T(8,128)(2,1)}, u32[]{:S(2)}, u32[]{:S(2)}) %collective-permute-start) | collective-permute-done | bytes 2097184 | tf_op jit(solution)/shard_map/ppermute | solution.py:13
  62.7 4.6 %broadcast_select_fusion.2 = (bf16[4096,256]{1,0:T(8,128)(2,1)S(1)}, bf16[4096,256]{1,0:T(8,128)(2,1)}, bf16[4096,256]{1,0:T(8,128)(2,1)}) fusion(bf16[4096,256]{1,0:T(8,128)(2,1)} %all-gather.2.cloned.1.call-done, bf16[4096,256]{1,0:T(8,128)(2,1)} %collective-permute-done, pred[]{:T(512)S(6)} %eq.6, pred[]{:T(512)S(6)} %eq.12), kind=kLoop, calls=%fused_computation.10 | loop fusion | flops 3145728 | bytes 10485762 | tf_op jit(solution)/shard_map/jit(_where)/select_n | solution.py:31
  67.5 50.2 %all-reduce.5.cloned.1.call-done = bf16[4096,256]{1,0:T(8,128)(2,1)} async-done(((bf16[4096,256]{1,0:T(8,128)(2,1)}), bf16[4096,256]{1,0:T(8,128)(2,1)}) %all-reduce.5.cloned.1.call-update) | async-done | bytes 2097168 | tf_op jit(solution)/shard_map/psum | solution.py:18
  117.7 1.3 convolution_convert_fusion.1
  119.0 4.3 %fusion = bf16[256,8192]{1,0:T(8,128)(2,1)S(1)} fusion(bf16[256,256]{1,0:T(8,128)(2,1)S(1)} %convolution_convert_fusion.1, bf16[2,1,256,8192]{3,2,1,0:T(8,128)(2,1)} %param.4, bf16[4096,256]{1,0:T(8,128)(2,1)} %get-tuple-element.7, bf16[4096,256]{1,0:T(8,128)(2,1)S(1)} %get-tuple-element.6), kind=kOutput, calls=%fused_computation.3 | convolution fusion | flops 1088421888 | bytes 12713984 | tf_op jit(solution)/shard_map/dot_general | solution.py:46
  123.2 1.5 convolution_convert_fusion
  124.7 9.4 %fusion.1 = bf16[256,8192]{1,0:T(8,128)(2,1)S(1)} fusion(bf16[256,256]{1,0:T(8,128)(2,1)S(1)} %convolution_convert_fusion, bf16[2,1,256,8192]{3,2,1,0:T(8,128)(2,1)} %param.4, bf16[4096,256]{1,0:T(8,128)(2,1)S(1)} %copy-done.6, bf16[4096,256]{1,0:T(8,128)(2,1)S(1)} %get-tuple-element.6), kind=kOutput, calls=%fused_computation.4 | convolution fusion | flops 1088421888 | bytes 12713984 | tf_op jit(solution)/shard_map/dot_general | solution.py:46
  134.2 1.3 fusion.43
  135.5 0.7 copy-done.2
  136.2 1.3 convolution_add_fusion
  137.5 2.8 slice_select_fusion
  140.3 1.7 copy-done
  142.0 4.2 %fusion.41 = f32[256,256]{1,0:T(8,128)S(1)} fusion(bf16[256,8192]{1,0:T(8,128)(2,1)} %copy-done.4, bf16[4096,256]{1,0:T(8,128)(2,1)} %get-tuple-element.7, bf16[4096,256]{1,0:T(8,128)(2,1)S(1)} %get-tuple-element.6), kind=kOutput, calls=%fused_computation.61 | convolution fusion | flops 1082130432 | bytes 8650752 | tf_op jit(solution)/shard_map/dot_general | solution.py:53
  146.2 1.2 fusion.24
  147.5 1.2 fusion.40
  148.7 1.9 multiply_add_fusion
  150.9 0.5 fusion.7
  151.5 0.5 fusion.2
  152.0 0.8 copy-done.5
  152.8 33.6 %all-reduce.7.cloned.1.call-done = f32[256,256]{1,0:T(8,128)} async-done(((f32[256,256]{1,0:T(8,128)}), f32[256,256]{1,0:T(8,128)}) %all-reduce.7.cloned.1.call-update) | async-done | bytes 262160 | tf_op jit(solution)/shard_map/psum | solution.py:73
  186.4 24.1 %reduce-scatter.5.cloned.1.call-done = f32[128,256]{1,0:T(8,128)} async-done(((f32[512,256]{1,0:T(8,128)}), f32[128,256]{1,0:T(8,128)}) %reduce-scatter.5.cloned.1.call-update) | async-done | bytes 131088 | tf_op jit(solution)/shard_map/reduce_scatter | solution.py:71
  210.6 7.4 %select_add_fusion = f32[4096,256]{1,0:T(8,128)} fusion(f32[4096,256]{1,0:T(8,128)} %collective-permute-done.1, f32[8192,256]{1,0:T(8,128)} %copy-done, pred[]{:T(512)S(6)} %eq.6), kind=kLoop, calls=%fused_computation.6 | loop fusion | flops 2097152 | bytes 16777216 | tf_op jit(solution)/shard_map/add | solution.py:67
  218.6 0.3 fusion.17
  219.2 5.7 %psum.39 = f32[2,256]{1,0:T(2,128)S(1)} all-reduce(f32[2,256]{1,0:T(2,128)S(1)} %pad_maximum_fusion.1), channel_id=1, replica_groups=mesh['groups'=2,'tile'=4,'cuts'=4] {'tile'}, use_global_device_ids=true, to_apply=%region_6.7 | all-reduce | flops 512 | bytes 4096 | tf_op jit(solution)/shard_map/psum | solution.py:74
  224.9 0.6 broadcast_multiply_fusion.3
  225.5 18.3 %all-reduce.9.cloned.1.call-done = (f32[128,256]{1,0:T(8,128)}, f32[256,256]{1,0:T(8,128)}) async-done(((f32[128,256]{1,0:T(8,128)}, f32[256,256]{1,0:T(8,128)}), (f32[128,256]{1,0:T(8,128)}, f32[256,256]{1,0:T(8,128)})) %all-reduce.9.cloned.1.call-update) | async-done | bytes 393232 | tf_op jit(solution)/shard_map/psum | solution.py:72
  243.8 1.6 broadcast_multiply_fusion.2
  245.4 1.7 broadcast_multiply_fusion.1
  247.1 75.8 %reduce-scatter.3.cloned.1.call-done = f32[1024,256]{1,0:T(8,128)} async-done(((f32[4096,256]{1,0:T(8,128)}), f32[1024,256]{1,0:T(8,128)}) %reduce-scatter.3.cloned.1.call-update) | async-done | bytes 1048592 | tf_op jit(solution)/shard_map/reduce_scatter | solution.py:67
  322.9 2.3 broadcast_multiply_fusion
  (37 shorter events, 1.5 us)
Async XLA Ops:
  7.2 51.1 %all-gather.2.cloned.1.call-start = ((), (), s32[]{:S(2)}) async-start(), calls=%async_computation.2 | async-start | bytes 2621440 | tf_op jit(solution)/shard_map/all_gather | solution.py:28
  7.9 109.8 %all-reduce.5.cloned.1.call-start = ((), (), s32[]{:S(2)}) async-start(), calls=%async_computation.3 | async-start | bytes 4194304 | tf_op jit(solution)/shard_map/psum | solution.py:18
  58.2 4.5 %collective-permute-start = (bf16[4096,256]{1,0:T(8,128)(2,1)}, bf16[4096,256]{1,0:T(8,128)(2,1)}, u32[]{:S(2)}, u32[]{:S(2)}) collective-permute-start(bf16[4096,256]{1,0:T(8,128)(2,1)} %all-gather.2.cloned.1.call-done), channel_id=1, source_target_pairs={{0,4},{4,0},{8,12},{12,8},{1,5},{5,1},{9,13},{13,9},{2,6},{6,2},{1... | collective-permute-start | bytes 6291464 | tf_op jit(solution)/shard_map/ppermute | solution.py:13
  58.2 9.2 %copy-start.8 = (f32[2,256]{1,0:T(2,128)S(1)}, f32[2,256]{1,0:T(2,128)}, u32[]{:S(2)}) copy-start(f32[2,256]{1,0:T(2,128)} %param.6) | copy-start | bytes 6148
  58.2 59.4 %copy-start.1 = (f32[256,256]{1,0:T(8,128)S(1)}, f32[256,256]{1,0:T(8,128)}, u32[]{:S(2)}) copy-start(f32[256,256]{1,0:T(8,128)} %param.7) | copy-start | bytes 786436
  67.4 119.0 %all-reduce.7.cloned.1.call-start = ((), (), s32[]{:S(2)}) async-start(), calls=%async_computation.6 | async-start | bytes 524288 | tf_op jit(solution)/shard_map/psum | solution.py:73
  119.0 5.8 %copy-start.6 = (bf16[4096,256]{1,0:T(8,128)(2,1)S(1)}, bf16[4096,256]{1,0:T(8,128)(2,1)}, u32[]{:S(2)}) copy-start(bf16[4096,256]{1,0:T(8,128)(2,1)} %get-tuple-element.7) | copy-start | bytes 6291460
  123.2 10.9 %copy-start.4 = (bf16[256,8192]{1,0:T(8,128)(2,1)}, bf16[256,8192]{1,0:T(8,128)(2,1)S(1)}, u32[]{:S(2)}) copy-start(bf16[256,8192]{1,0:T(8,128)(2,1)S(1)} %fusion) | copy-start | bytes 12582916
  134.2 2.0 copy-start.2
  137.5 4.5 %copy-start = (f32[8192,256]{1,0:T(8,128)}, f32[8192,256]{1,0:T(8,128)S(1)}, u32[]{:S(2)}) copy-start(f32[8192,256]{1,0:T(8,128)S(1)} %convolution_add_fusion) | copy-start | bytes 25165828
  142.0 68.6 %collective-permute-start.1 = (f32[4096,256]{1,0:T(8,128)}, f32[4096,256]{1,0:T(8,128)}, u32[]{:S(2)}, u32[]{:S(2)}) collective-permute-start(f32[4096,256]{1,0:T(8,128)} %slice_select_fusion), channel_id=1, source_target_pairs={{0,4},{4,0},{8,12},{12,8},{1,5},{5,1},{9,13},{13,9},{2,6},{6,2},{1... | collective-permute-start | bytes 12582920 | tf_op jit(solution)/shard_map/ppermute | solution.py:13
  142.0 5.5 %copy-start.3 = (bf16[256,8192]{1,0:T(8,128)(2,1)S(1)}, bf16[256,8192]{1,0:T(8,128)(2,1)}, u32[]{:S(2)}) copy-start(bf16[256,8192]{1,0:T(8,128)(2,1)} %copy-done.2) | copy-start | bytes 12582916
  142.0 5.5 %copy-start.7 = (bf16[4096,256]{1,0:T(8,128)(2,1)S(1)}, bf16[4096,256]{1,0:T(8,128)(2,1)}, u32[]{:S(2)}) copy-start(bf16[4096,256]{1,0:T(8,128)(2,1)} %get-tuple-element.7) | copy-start | bytes 6291460
  150.7 59.8 %reduce-scatter.5.cloned.1.call-start = ((), (), s32[]{:S(2)}) async-start(), calls=%async_computation.5 | async-start | bytes 655360 | tf_op jit(solution)/shard_map/reduce_scatter | solution.py:71
  152.0 0.8 copy-start.5
  152.8 91.0 %all-reduce.9.cloned.1.call-start = ((), (), s32[]{:S(2)}) async-start(), calls=%async_computation.7 | async-start | bytes 786432 | tf_op jit(solution)/shard_map/psum | solution.py:72
  210.6 112.3 %reduce-scatter.3.cloned.1.call-start = ((), (), s32[]{:S(2)}) async-start(), calls=%async_computation.4 | async-start | bytes 5242880 | tf_op jit(solution)/shard_map/reduce_scatter | solution.py:67
Sparse Core Ops, SparseCore 0:
  9.6 48.6 all-gather.1
  67.5 50.0 all-reduce.4
  150.8 35.5 all-reduce.6
  189.1 21.3 reduce-scatter.4
  212.8 30.9 all-reduce.8
  246.1 76.7 reduce-scatter.2
